TPU v7x, 1024 devices: a whole 8x8x8 slice. The times are simulated.
1024 devices in a mesh: row: 16 (over y_hi, x), col: 16 (over z, core), rep: 4 (over y_lo).
Axes of the slice: x: 8, y: 8 (y_hi: 2, y_lo: 4; y = y_hi * 4 + y_lo), z: 8, core: 2. Of those that a mesh axis runs over, the one named last changes fastest.
Arguments:
- a_blocks: float32 [16, 16, 4, 16, 128, 128], P('row', 'col', 'rep'), may hold values from -6 to 6
- a_where: int32 [16, 16, 4, 16], P('row', 'col', 'rep'), may hold values from 0 to 255, as said below
- b_blocks: float32 [16, 16, 4, 32, 128, 128], P('row', 'col', 'rep'), may hold values from -0.09375 to 0.09375
- b_where: int32 [16, 16, 4, 32], P('row', 'col', 'rep'), may hold values from 0 to 255, as said below
- c_where: int32 [16, 16, 8], P('row', 'col'), may hold values from 0 to 15, as said below
Outputs:
- c_blocks: float32 [16, 16, 8, 128, 128], P('row', 'col', 'rep')
Inputs may be any that keep to these rules, and one draw needn't show every extreme that they name: `a_where`: within one device's list the positions are distinct. Panels (left and right) with the same replica and the same (p + q) mod 16 draw their inner block indices from one common set of 8; each left block row holds 4 blocks of that set, and a right panel holds all 4 blocks of each of its 8 inner block rows. List order is arbitrary. `b_where`: within one device's list the positions are distinct; see a_where for the inner index sets. `c_where`: within one panel's list the positions are distinct.
All inputs are finite; a program needn't handle non-finite values.
Results may differ from a plain program's by a relative error of at most 0.0003.
Values sent between devices are 32-bit elements; how exact they have to be, the bound alone decides.
A program may use at most 32 MiB of HBM per device.

v0:
```python
import jax
import jax.numpy as jnp
from jax import lax
from jax.sharding import PartitionSpec as P

KB = 64
CB = 4


def from_behind(shard, axis, by):
    peers = lax.axis_size(axis)
    return lax.ppermute(shard, axis, [(i, (i + by) % peers) for i in range(peers)])


def kept_product(a_list, a_spots, b_list, b_spots, c_spots):
    a_inner = a_spots % KB
    a_row = a_spots // KB
    b_inner = b_spots // CB
    b_col = b_spots % CB
    columns = jnp.arange(CB, dtype=jnp.int32)
    pick = (
        (a_inner[:, None, None] == b_inner[None, None, :])
        & (b_col[None, None, :] == columns[None, :, None])
    ).astype(jnp.float32)
    matched = jnp.einsum("ajb,bxy->ajxy", pick, b_list, precision=lax.Precision.HIGHEST)
    pieces = jnp.einsum("axy,ajyz->ajxz", a_list, matched, precision=lax.Precision.HIGHEST)
    keep = (
        ((c_spots // CB)[:, None, None] == a_row[None, :, None])
        & ((c_spots % CB)[:, None, None] == columns[None, None, :])
    ).astype(jnp.float32)
    return jnp.einsum("saj,ajxz->sxz", keep, pieces, precision=lax.Precision.HIGHEST)


def shards(a_blocks, a_where, b_blocks, b_where, c_where):
    a_list = a_blocks[0, 0, 0]
    a_spots = a_where[0, 0, 0]
    b_list = b_blocks[0, 0, 0]
    b_spots = b_where[0, 0, 0]
    c_spots = c_where[0, 0]
    a_later, a_later_spots = from_behind((a_list, a_spots), "col", -1)
    b_later, b_later_spots = from_behind((b_list, b_spots), "row", -1)
    first = kept_product(a_list, a_spots, b_list, b_spots, c_spots)
    second = kept_product(a_later, a_later_spots, b_later, b_later_spots, c_spots)
    share = lax.psum_scatter(first + second, "rep", scatter_dimension=0, tiled=True)
    return share[None, None]


def solution(mesh):
    in_specs = (
        P("row", "col", "rep", None, None, None),
        P("row", "col", "rep", None),
        P("row", "col", "rep", None, None, None),
        P("row", "col", "rep", None),
        P("row", "col", None),
    )
    out_specs = P("row", "col", "rep", None, None)
    return jax.shard_map(shards, mesh=mesh, in_specs=in_specs, out_specs=out_specs, check_vma=False)
```

profile of v0, /device:TPU:14, one launch (start us, length us, event | category | flops | bytes accessed | tf_op | source)
XLA Modules:
  0.0 183.4 jit_solution(9697292049681332329)
XLA Ops:
  6.5 0.0 copy-start
  6.5 0.0 reduce-scatter.2.cloned.1.call-start
  6.5 14.8 %collective-permute-start = (s32[16]{0:T(128)}, s32[16]{0:T(128)S(1)}, u32[]{:S(2)}, u32[]{:S(2)}) collective-permute-start(s32[16]{0:T(128)} %bitcast.80), channel_id=1, source_target_pairs={{0,60},{4,0},{8,4},{12,8},{16,12},{20,16},{24,20},{28,24},{32,28},... | collective-permute-start | bytes 200 | tf_op jit(solution)/shard_map/ppermute | solution.py:12
  21.4 3.3 %collective-permute-start.1 = (s32[32]{0:T(128)}, s32[32]{0:T(128)S(1)}, u32[]{:S(2)}, u32[]{:S(2)}) collective-permute-start(s32[32]{0:T(128)} %bitcast.81), channel_id=1, source_target_pairs={{0,960},{64,0},{128,64},{192,128},{256,192},{320,256},{384,320},{4... | collective-permute-start | bytes 392 | tf_op jit(solution)/shard_map/ppermute | solution.py:12
  24.7 3.3 %collective-permute-start.2 = (f32[32,128,128]{2,1,0:T(8,128)}, f32[32,128,128]{2,1,0:T(8,128)S(1)}, u32[]{:S(2)}, u32[]{:S(2)}) collective-permute-start(f32[32,128,128]{2,1,0:T(8,128)} %bitcast.76), channel_id=1, source_target_pairs={{0,960},{64,0},{128,64},{192,128},{256,192},{320,256},{384,320},{4... | collective-permute-start | bytes 6291464 | tf_op jit(solution)/shard_map/ppermute | solution.py:12
  28.1 0.1 collective-permute-start.3
  28.2 0.7 and_select_fusion.8
  28.9 0.7 and_select_fusion.5
  29.5 0.7 and_select_fusion.9
  30.2 0.1 broadcast_compare_fusion.1
  30.3 4.8 %fusion.10 = f32[16,4,128,128]{3,0,2,1:T(8,128)S(1)} fusion(f32[32,128,128,1]{2,1,0,3:T(8,128)} %bitcast.77, pred[16,4,32,1]{2,1,0,3:T(4,128)(4,1)S(1)} %and_bitcast_fusion.1), kind=kOutput, calls=%fused_computation.10 | convolution fusion | flops 402653184 | bytes 6293504 | tf_op jit(solution)/shard_map/ajb,bxy->ajxy/dot_general | solution.py:25
  35.1 0.0 copy-done
  35.1 9.6 %fusion.6 = f32[16,4,128,128]{3,2,1,0:T(8,128)} fusion(f32[16,4,128,128]{3,0,2,1:T(8,128)S(1)} %fusion.10, f32[1,1,1,16,128,128]{5,4,3,2,1,0:T(8,128)S(1)} %copy-done), kind=kOutput, calls=%fused_computation.6 | convolution fusion | flops 1610612736 | bytes 9437184 | tf_op jit(solution)/shard_map/axy,ajyz->ajxz/dot_general | solution.py:26
  44.7 5.5 %copy.12 = f32[16,4,128,128]{2,0,1,3:T(8,128)} copy(f32[16,4,128,128]{3,2,1,0:T(8,128)} %fusion.6) | data formatting | bytes 8388608 | tf_op jit(solution)/shard_map/axy,ajyz->ajxz/dot_general | solution.py:26
  50.2 0.0 collective-permute-done
  50.2 0.1 broadcast_compare_fusion.2
  50.3 4.4 %fusion.12 = f32[8,128,128]{2,0,1:T(8,128)S(1)} fusion(f32[16,4,128,128]{2,0,1,3:T(8,128)} %copy.12, pred[8,4]{0,1:T(4,128)(4,1)S(1)} %iota_compare_fusion.2, pred[8,16]{1,0:T(8,128)(4,1)S(1)} %get-tuple-element.6), kind=kOutput, calls=%fused_computation.12 | convolution fusion | flops 100663808 | bytes 4718752 | tf_op jit(solution)/shard_map/saj,ajxz->sxz/dot_general | solution.py:31
  54.7 0.0 collective-permute-done.1
  54.7 0.1 broadcast_compare_fusion
  54.8 57.5 %collective-permute-done.2 = f32[32,128,128]{2,1,0:T(8,128)S(1)} collective-permute-done((f32[32,128,128]{2,1,0:T(8,128)}, f32[32,128,128]{2,1,0:T(8,128)S(1)}, u32[]{:S(2)}, u32[]{:S(2)}) %collective-permute-start.2) | collective-permute-done | bytes 2097184 | tf_op jit(solution)/shard_map/ppermute | solution.py:12
  112.3 3.3 %fusion.8 = f32[16,4,128,128]{3,0,2,1:T(8,128)S(1)} fusion(f32[32,128,128,1]{2,1,0,3:T(8,128)S(1)} %bitcast.78, pred[16,4,32,1]{2,1,0,3:T(4,128)(4,1)S(1)} %and_bitcast_fusion), kind=kOutput, calls=%fused_computation.8 | convolution fusion | flops 402653184 | bytes 6293504 | tf_op jit(solution)/shard_map/ajb,bxy->ajxy/dot_general | solution.py:25
  115.6 0.0 collective-permute-done.3
  115.6 10.7 %fusion.4 = f32[16,4,128,128]{3,2,1,0:T(8,128)} fusion(f32[16,4,128,128]{3,0,2,1:T(8,128)S(1)} %fusion.8, f32[16,128,128]{2,1,0:T(8,128)} %collective-permute-done.3), kind=kOutput, calls=%fused_computation.4 | convolution fusion | flops 1610612736 | bytes 9437184 | tf_op jit(solution)/shard_map/axy,ajyz->ajxz/dot_general | solution.py:26
  126.2 5.5 %copy.18 = f32[16,4,128,128]{2,0,1,3:T(8,128)} copy(f32[16,4,128,128]{3,2,1,0:T(8,128)} %fusion.4) | data formatting | bytes 8388608 | tf_op jit(solution)/shard_map/axy,ajyz->ajxz/dot_general | solution.py:26
  131.7 4.4 %fusion.18 = f32[8,128,128]{2,0,1:T(8,128)S(1)} fusion(f32[8,128,128]{2,0,1:T(8,128)S(1)} %fusion.12, f32[16,4,128,128]{2,0,1,3:T(8,128)} %copy.18, pred[8,16]{1,0:T(8,128)(4,1)S(1)} %get-tuple-element.5, pred[8,4]{0,1:T(4,128)(4,1)S(1)} %iota_compare_fusion.2), kind=kOutput, calls=%fused_computation.14 | convolution fusion | flops 100794880 | bytes 5243040 | tf_op jit(solution)/shard_map/saj,ajxz->sxz/dot_general | solution.py:31
  136.1 0.9 copy.7
  137.0 0.0 reduce-scatter.2.cloned.1.call-update
  137.0 39.5 %reduce-scatter.2.cloned.1.call-done = f32[2,128,128]{2,1,0:T(8,128)} async-done(((f32[8,128,128]{2,1,0:T(8,128)}), f32[2,128,128]{2,1,0:T(8,128)}) %reduce-scatter.2.cloned.1.call-update) | async-done | bytes 131088 | tf_op jit(solution)/shard_map/reduce_scatter | solution.py:44
  (7 shorter events, 0.1 us)
Async XLA Ops:
  6.5 28.6 %copy-start = (f32[1,1,1,16,128,128]{5,4,3,2,1,0:T(8,128)S(1)}, f32[1,1,1,16,128,128]{5,4,3,2,1,0:T(8,128)}, u32[]{:S(2)}) copy-start(f32[1,1,1,16,128,128]{5,4,3,2,1,0:T(8,128)} %param.5) | copy-start | bytes 3145732
  6.5 170.0 %reduce-scatter.2.cloned.1.call-start = ((), (), s32[]{:S(2)}) async-start(), calls=%async_computation.1 | async-start | bytes 655360 | tf_op jit(solution)/shard_map/reduce_scatter | solution.py:44
  6.5 43.6 %collective-permute-start = (s32[16]{0:T(128)}, s32[16]{0:T(128)S(1)}, u32[]{:S(2)}, u32[]{:S(2)}) collective-permute-start(s32[16]{0:T(128)} %bitcast.80), channel_id=1, source_target_pairs={{0,60},{4,0},{8,4},{12,8},{16,12},{20,16},{24,20},{28,24},{32,28},... | collective-permute-start | bytes 200 | tf_op jit(solution)/shard_map/ppermute | solution.py:12
  21.4 33.3 %collective-permute-start.1 = (s32[32]{0:T(128)}, s32[32]{0:T(128)S(1)}, u32[]{:S(2)}, u32[]{:S(2)}) collective-permute-start(s32[32]{0:T(128)} %bitcast.81), channel_id=1, source_target_pairs={{0,960},{64,0},{128,64},{192,128},{256,192},{320,256},{384,320},{4... | collective-permute-start | bytes 392 | tf_op jit(solution)/shard_map/ppermute | solution.py:12
  24.7 87.6 %collective-permute-start.2 = (f32[32,128,128]{2,1,0:T(8,128)}, f32[32,128,128]{2,1,0:T(8,128)S(1)}, u32[]{:S(2)}, u32[]{:S(2)}) collective-permute-start(f32[32,128,128]{2,1,0:T(8,128)} %bitcast.76), channel_id=1, source_target_pairs={{0,960},{64,0},{128,64},{192,128},{256,192},{320,256},{384,320},{4... | collective-permute-start | bytes 6291464 | tf_op jit(solution)/shard_map/ppermute | solution.py:12
  28.1 87.5 %collective-permute-start.3 = (f32[16,128,128]{2,1,0:T(8,128)}, f32[16,128,128]{2,1,0:T(8,128)}, u32[]{:S(2)}, u32[]{:S(2)}) collective-permute-start(f32[16,128,128]{2,1,0:T(8,128)} %bitcast.79), channel_id=1, source_target_pairs={{0,60},{4,0},{8,4},{12,8},{16,12},{20,16},{24,20},{28,24},{32,28},... | collective-permute-start | bytes 3145736 | tf_op jit(solution)/shard_map/ppermute | solution.py:12
Sparse Core Ops, SparseCore 0:
  137.2 39.3 reduce-scatter.1
where the time goes:
time: 184 us; the launch traced here: 183 us
  waiting for transfers between devices  97 us (53%)
  matrix products  37.1 us (20%)
  starting transfers between devices  21.7 us (12%)
  between operations  13.5 us (7%)
  local copies, waits for them, and re-layouts  11.9 us (6%)
  other arithmetic  2.29 us (1%)
    ppermute x4, waiting for transfers between devices, from_behind(): lax.ppermute(shard, axis, [(i, (i + by) % peers) for i in range(peers)])  57.5 us
    reduce_scatter x1, waiting for transfers between devices, shards(): lax.psum_scatter(first + second, 'rep', scatter_dimension=0, tiled=True)  39.5 us
    ppermute x4, starting transfers between devices, from_behind(): lax.ppermute(shard, axis, [(i, (i + by) % peers) for i in range(peers)])  21.6 us
    dot_general x2, matrix products, kept_product(): jnp.einsum('axy,ajyz->ajxz', a_list, matched, precision=lax.Precision.HIG...  20.2 us
    dot_general x2, local copies, waits for them, and re-layouts, kept_product(): jnp.einsum('axy,ajyz->ajxz', a_list, matched, precision=lax.Precision.HIG...  11 us
    dot_general x2, matrix products, kept_product(): jnp.einsum('saj,ajxz->sxz', keep, pieces, precision=lax.Precision.HIGHEST)  8.79 us
    dot_general x2, matrix products, kept_product(): jnp.einsum('ajb,bxy->ajxy', pick, b_list, precision=lax.Precision.HIGHEST)  8.06 us
  transfers between devices with their start and end apart: 5, of which 2 were waited for; matrix products, arithmetic and copies ran while one was open for 16% of the time, Pallas kernels for 0%

commit v1 on v0

v1 whole, which is shorter than its diff:
```python
import functools

import jax
import jax.numpy as jnp
from jax import lax
from jax.experimental import pallas as pl
from jax.experimental.pallas import tpu as pltpu
from jax.sharding import PartitionSpec as P

KB = 64
CB = 4
RB = 4
KSET = 8
NA = 16
NB = 32
NC = 8
BLOCK = 128
CHUNKS = 4
PER_CHUNK = NA // CHUNKS
MESH = pl.DeviceIdType.MESH


def sort_order(where, count, rank, order):
    def rank_one(n, carry):
        mine = where[0, n]
        below = jnp.int32(0)
        for m in range(count):
            below += (where[0, m] < mine).astype(jnp.int32)
        rank[n] = below
        return carry

    lax.fori_loop(0, count, rank_one, 0)

    def place_one(t, carry):
        found = jnp.int32(0)
        for n in range(count):
            found = jnp.where(rank[n] == t, n, found)
        order[t] = found
        return carry

    lax.fori_loop(0, count, place_one, 0)


def split(x):
    high = x.astype(jnp.bfloat16)
    low = (x - high.astype(jnp.float32)).astype(jnp.bfloat16)
    return high, low


def kernel(
    rows, cols, reps,
    a_where, b_where, c_where, a_hbm, b_hbm, aw_hbm, cw_hbm, out,
    a_own, b_own, a_next, aw_land, cw_land, aw_next, cw_next, right, pieces, first, second, got_first, got_second,
    rank, a_order, b_order, inner,
    local_sem, meta_sem, small_send, small_recv, a_send, a_recv, first_send, first_recv, second_send, second_recv,
):
    p, q, r = lax.axis_index("row"), lax.axis_index("col"), lax.axis_index("rep")
    p_up, p_down = lax.rem(p + 1, rows), lax.rem(p + rows - 1, rows)
    q_up, q_down = lax.rem(q + 1, cols), lax.rem(q + cols - 1, cols)
    share = NC // reps

    load_a = pltpu.make_async_copy(a_hbm, a_own, local_sem.at[0])
    load_b = pltpu.make_async_copy(b_hbm, b_own, local_sem.at[1])
    load_b.start()
    load_a.start()

    barrier = pltpu.get_barrier_semaphore()
    pl.semaphore_signal(barrier, inc=1, device_id=(p_down, q_up, r), device_id_type=MESH)
    pl.semaphore_signal(barrier, inc=1, device_id=(p_down, q, r), device_id_type=MESH)
    for d in range(reps):
        there = lax.rem(r + d, reps)
        pl.semaphore_signal(barrier, inc=1, device_id=(p_up, q, there), device_id_type=MESH)
        if d:
            pl.semaphore_signal(barrier, inc=1, device_id=(p, q, there), device_id_type=MESH)
    pl.semaphore_wait(barrier, 2 * reps + 1)

    away = (p_up, q_down, r)
    small = [
        pltpu.make_async_remote_copy(
            src_ref=aw_hbm, dst_ref=aw_land, send_sem=small_send.at[0], recv_sem=small_recv.at[0],
            device_id=away, device_id_type=MESH,
        ),
        pltpu.make_async_remote_copy(
            src_ref=cw_hbm, dst_ref=cw_land, send_sem=small_send.at[1], recv_sem=small_recv.at[1],
            device_id=(p_up, q, r), device_id_type=MESH,
        ),
    ]
    for copy in small:
        copy.start()
    panels = []
    for c in range(CHUNKS):
        part = pl.ds(c * PER_CHUNK, PER_CHUNK)
        copy = pltpu.make_async_remote_copy(
            src_ref=a_hbm.at[part], dst_ref=a_next.at[part], send_sem=a_send.at[c], recv_sem=a_recv.at[c],
            device_id=away, device_id_type=MESH,
        )
        copy.start()
        panels.append(copy)

    sort_order(b_where, NB, rank, b_order)
    load_b.wait()

    def lay_right(u, carry):
        for j in range(CB):
            high, low = split(b_own[b_order[u * CB + j]])
            at = slice(j * BLOCK, (j + 1) * BLOCK)
            right[u, :BLOCK, at] = high
            right[u, BLOCK:, at] = low
        return carry

    lax.fori_loop(0, KSET, lay_right, 0)

    def places(where):
        def one(n, carry):
            k = lax.rem(where[0, n], KB)
            slot = jnp.int32(0)
            for u in range(1, KSET):
                slot += (b_where[0, b_order[u * CB]] <= k * CB).astype(jnp.int32)
            inner[n] = slot
            return carry

        lax.fori_loop(0, NA, one, 0)
        sort_order(where, NA, rank, a_order)

    def multiply(blocks):
        def one(n, carry):
            high, low = split(blocks[n])
            left = jnp.concatenate(
                [jnp.concatenate([high, high], axis=1), jnp.concatenate([low, low], axis=1)], axis=0
            )
            both = jnp.dot(left, right[inner[n]], preferred_element_type=jnp.float32)
            total = both[:BLOCK] + both[BLOCK:]
            for j in range(CB):
                pieces[n * CB + j] = total[:, j * BLOCK:(j + 1) * BLOCK]
            return carry

        return one

    def keep(spots, into, s):
        spot = spots[0, s]
        i, j = spot // CB, lax.rem(spot, CB)
        total = pieces[a_order[i * RB] * CB + j]
        for t in range(1, RB):
            total += pieces[a_order[i * RB + t] * CB + j]
        into[s] = total

    places(a_where)
    load_a.wait()
    lax.fori_loop(0, NA, multiply(a_own), 0)

    def keep_first(s, carry):
        keep(c_where, first, s)
        return carry

    lax.fori_loop(0, NC, keep_first, 0)
    firsts = []
    for d in range(1, reps):
        there = lax.rem(r + d, reps)
        copy = pltpu.make_async_remote_copy(
            src_ref=first.at[pl.ds(there * share, share)], dst_ref=got_first.at[d - 1],
            send_sem=first_send.at[d - 1], recv_sem=first_recv.at[d - 1],
            device_id=(p, q, there), device_id_type=MESH,
        )
        copy.start()
        firsts.append(copy)

    for copy in small:
        copy.wait_recv()
    to_scalars = [
        pltpu.make_async_copy(aw_land, aw_next, meta_sem.at[0]),
        pltpu.make_async_copy(cw_land, cw_next, meta_sem.at[1]),
    ]
    for copy in to_scalars:
        copy.start()
    for copy in to_scalars:
        copy.wait()
    places(aw_next)
    for c in range(CHUNKS):
        panels[c].wait_recv()
        lax.fori_loop(c * PER_CHUNK, (c + 1) * PER_CHUNK, multiply(a_next), 0)
    seconds = []
    for d in range(reps):
        there = lax.rem(r + d, reps)

        def keep_second(s, carry):
            keep(cw_next, second, there * share + s)
            return carry

        lax.fori_loop(0, share, keep_second, 0)
        copy = pltpu.make_async_remote_copy(
            src_ref=second.at[pl.ds(there * share, share)], dst_ref=got_second.at[d],
            send_sem=second_send.at[d], recv_sem=second_recv.at[d],
            device_id=(p_down, q, there), device_id_type=MESH,
        )
        copy.start()
        seconds.append(copy)

    total = first[pl.ds(r * share, share)]
    for d in range(1, reps):
        firsts[d - 1].wait_recv()
        total += got_first[d - 1]
    for d in range(reps):
        seconds[d].wait_recv()
        total += got_second[d]
    out[...] = total
    for copy in small + panels + firsts + seconds:
        copy.wait_send()


def shards(rows, cols, reps, a_blocks, a_where, b_blocks, b_where, c_where):
    share = NC // reps
    a_spots = a_where.reshape(1, NA)
    b_spots = b_where.reshape(1, NB)
    c_spots = c_where.reshape(1, NC)
    smem, hbm, vmem = (pl.BlockSpec(memory_space=m) for m in (pltpu.SMEM, pl.ANY, pltpu.VMEM))
    dma = pltpu.SemaphoreType.DMA
    f32, i32, bf16 = jnp.float32, jnp.int32, jnp.bfloat16
    result = pl.pallas_call(
        functools.partial(kernel, rows, cols, reps),
        out_shape=jax.ShapeDtypeStruct((share, BLOCK, BLOCK), f32),
        in_specs=[smem, smem, smem, hbm, hbm, hbm, hbm],
        out_specs=vmem,
        scratch_shapes=[
            pltpu.VMEM((NA, BLOCK, BLOCK), f32),
            pltpu.VMEM((NB, BLOCK, BLOCK), f32),
            pltpu.VMEM((NA, BLOCK, BLOCK), f32),
            pltpu.VMEM((1, NA), i32),
            pltpu.VMEM((1, NC), i32),
            pltpu.SMEM((1, NA), i32),
            pltpu.SMEM((1, NC), i32),
            pltpu.VMEM((KSET, 2 * BLOCK, CB * BLOCK), bf16),
            pltpu.VMEM((NA * CB, BLOCK, BLOCK), f32),
            pltpu.VMEM((NC, BLOCK, BLOCK), f32),
            pltpu.VMEM((NC, BLOCK, BLOCK), f32),
            pltpu.VMEM((reps - 1, share, BLOCK, BLOCK), f32),
            pltpu.VMEM((reps, share, BLOCK, BLOCK), f32),
            pltpu.SMEM((NB,), i32),
            pltpu.SMEM((NA,), i32),
            pltpu.SMEM((NB,), i32),
            pltpu.SMEM((NA,), i32),
            dma((2,)), dma((2,)), dma((2,)), dma((2,)), dma((CHUNKS,)), dma((CHUNKS,)),
            dma((reps - 1,)), dma((reps - 1,)), dma((reps,)), dma((reps,)),
        ],
        compiler_params=pltpu.CompilerParams(
            collective_id=0, has_side_effects=True, vmem_limit_bytes=60 * 1024 * 1024
        ),
        cost_estimate=pl.CostEstimate(flops=2 * 2 * NA * 4 * CB * BLOCK**3, bytes_accessed=4 << 20, transcendentals=0),
    )(
        a_spots, b_spots, c_spots,
        a_blocks.reshape(NA, BLOCK, BLOCK), b_blocks.reshape(NB, BLOCK, BLOCK), a_spots, c_spots,
    )
    return result[None, None]


def solution(mesh):
    in_specs = (
        P("row", "col", "rep", None, None, None),
        P("row", "col", "rep", None),
        P("row", "col", "rep", None, None, None),
        P("row", "col", "rep", None),
        P("row", "col", None),
    )
    out_specs = P("row", "col", "rep", None, None)
    body = functools.partial(shards, mesh.shape["row"], mesh.shape["col"], mesh.shape["rep"])
    return jax.shard_map(body, mesh=mesh, in_specs=in_specs, out_specs=out_specs, check_vma=False)
```

time: 184 us -> 95.7 us (0.52)
  the two profiles are of different devices: /device:TPU:14 before, /device:TPU:399 now
where the time goes in v1:
time: 95.7 us; the launch traced here: 95.5 us
  Pallas kernels  94 us (98%)
  local copies, waits for them, and re-layouts  1.57 us (2%)
    pallas_call x1, Pallas kernels, shards(): pl.pallas_call(functools.partial(kernel, rows, cols, reps), out_shape=jax...  94 us

profile of v1, /device:TPU:399, one launch (start us, length us, event | category | flops | bytes accessed | tf_op | source)
XLA Modules:
  0.0 95.5 jit_solution(5813493876437108445)
XLA Ops:
  0.0 94.0 %shard_map.55 = f32[2,128,128]{2,1,0:T(8,128)} custom-call(s32[1,16]{1,0:T(1,128)} %bitcast.9, s32[1,32]{1,0:T(1,128)} %bitcast.11, s32[1,8]{1,0:T(1,128)} %bitcast.12, f32[16,128,128]{2,1,0:T(8,128)} %bitcast.8, f32[32,128,128]{2,1,0:T(8,128)} %bitcast.7, s32[1,16]{1,0:T(1,128)} %bitcast.10, s32[1,8]{1,0:T(1,128)} %bitcast.13), custom_call_target="tpu_custom_call" | custom-call | flops 2147483648 | bytes 4194304 | tf_op jit(solution)/shard_map/pallas_call | solution.py:218
  94.0 1.6 %copy.7 = f32[1,1,2,128,128]{4,3,2,1,0:T(8,128)} copy(f32[1,1,2,128,128]{4,3,2,1,0:T(8,128)} %bitcast.6) | data formatting | bytes 262144

commit v2 on v1

--- a/solution.py
+++ b/solution.py
@@ -15,7 +15,7 @@
 NB = 32
 NC = 8
 BLOCK = 128
-CHUNKS = 4
+CHUNKS = 8
 PER_CHUNK = NA // CHUNKS
 MESH = pl.DeviceIdType.MESH
 
@@ -50,9 +50,9 @@
 def kernel(
     rows, cols, reps,
     a_where, b_where, c_where, a_hbm, b_hbm, aw_hbm, cw_hbm, out,
-    a_own, b_own, a_next, aw_land, cw_land, aw_next, cw_next, right, pieces, first, second, got_first, got_second,
+    a_own, b_own, a_next, via, aw_land, cw_land, aw_next, cw_next, right, pieces, first, second, got_first, got_second,
     rank, a_order, b_order, inner,
-    local_sem, meta_sem, small_send, small_recv, a_send, a_recv, first_send, first_recv, second_send, second_recv,
+    local_sem, meta_sem, small_send, small_recv, a_send, a_recv, via_send, via_recv, first_send, first_recv, second_send, second_recv,
 ):
     p, q, r = lax.axis_index("row"), lax.axis_index("col"), lax.axis_index("rep")
     p_up, p_down = lax.rem(p + 1, rows), lax.rem(p + rows - 1, rows)
@@ -64,38 +64,122 @@
     load_b.start()
     load_a.start()
 
+    width = rows // 2
+    x, half = lax.rem(p, width), p // width
+    last, stop, near = width - 1, width // 2, width // 8
+    across = lax.rem(p + width, rows)
+
+    def row_at(at, side):
+        return side * width + at
+
+    def remote(src, dst, send_sem, recv_sem, device):
+        return pltpu.make_async_remote_copy(
+            src_ref=src, dst_ref=dst, send_sem=send_sem, recv_sem=recv_sem, device_id=device, device_id_type=MESH
+        )
+
     barrier = pltpu.get_barrier_semaphore()
-    pl.semaphore_signal(barrier, inc=1, device_id=(p_down, q_up, r), device_id_type=MESH)
-    pl.semaphore_signal(barrier, inc=1, device_id=(p_down, q, r), device_id_type=MESH)
+
+    def greet(*device):
+        pl.semaphore_signal(barrier, inc=1, device_id=device, device_id_type=MESH)
+
+    greet(p_down, q_up, r)
+    greet(p_down, q, r)
     for d in range(reps):
         there = lax.rem(r + d, reps)
-        pl.semaphore_signal(barrier, inc=1, device_id=(p_up, q, there), device_id_type=MESH)
+        greet(p_up, q, there)
         if d:
-            pl.semaphore_signal(barrier, inc=1, device_id=(p, q, there), device_id_type=MESH)
-    pl.semaphore_wait(barrier, 2 * reps + 1)
+            greet(p, q, there)
+
+    @pl.when(x == last)
+    def _():
+        greet(across, q, r)
+
+    @pl.when(x == stop)
+    def _():
+        greet(row_at(last, 0), q, r)
+        greet(row_at(last, 1), q, r)
+
+    @pl.when(x == near)
+    def _():
+        greet(row_at(stop, 0), q, r)
+        greet(row_at(stop, 1), q, r)
+
+    @pl.when(x == 0)
+    def _():
+        greet(row_at(last, half), q_up, r)
+        greet(row_at(near, half), q_up, r)
+
+    more = jnp.where(x == last, 4, jnp.where(x == stop, 2, jnp.where(x == near, 1, 0)))
+    pl.semaphore_wait(barrier, 2 * reps + 1 + more)
 
     away = (p_up, q_down, r)
     small = [
-        pltpu.make_async_remote_copy(
-            src_ref=aw_hbm, dst_ref=aw_land, send_sem=small_send.at[0], recv_sem=small_recv.at[0],
-            device_id=away, device_id_type=MESH,
-        ),
-        pltpu.make_async_remote_copy(
-            src_ref=cw_hbm, dst_ref=cw_land, send_sem=small_send.at[1], recv_sem=small_recv.at[1],
-            device_id=(p_up, q, r), device_id_type=MESH,
-        ),
+        remote(aw_hbm, aw_land, small_send.at[0], small_recv.at[0], away),
+        remote(cw_hbm, cw_land, small_send.at[1], small_recv.at[1], (p_up, q, r)),
     ]
     for copy in small:
         copy.start()
-    panels = []
-    for c in range(CHUNKS):
-        part = pl.ds(c * PER_CHUNK, PER_CHUNK)
-        copy = pltpu.make_async_remote_copy(
-            src_ref=a_hbm.at[part], dst_ref=a_next.at[part], send_sem=a_send.at[c], recv_sem=a_recv.at[c],
-            device_id=away, device_id_type=MESH,
-        )
-        copy.start()
-        panels.append(copy)
+
+    def part(c):
+        return pl.ds(c * PER_CHUNK, PER_CHUNK)
+
+    panels = [
+        remote(a_hbm.at[part(c)], a_next.at[part(c)], a_send.at[c], a_recv.at[c], away) for c in range(CHUNKS)
+    ]
+
+    def leg(c, at, device):
+        return remote(a_hbm.at[part(c)], via.at[part(at)], a_send.at[c], via_recv.at[at], device)
+
+    def pass_on(at, device):
+        return remote(via.at[part(at)], via.at[part(at)], via_send.at[at], via_recv.at[at], device)
+
+    def land(at, c, device):
+        return remote(via.at[part(at)], a_next.at[part(c)], via_send.at[at], a_recv.at[c], device)
+
+    @pl.when(x != last)
+    def _():
+        for copy in panels:
+            copy.start()
+
+    @pl.when(x == last)
+    def _():
+        for c in range(2):
+            panels[c].start()
+            leg(2 + c, c, (across, q, r)).start()
+            leg(4 + c, c, (row_at(stop, 1 - half), q, r)).start()
+            leg(6 + c, 2 + c, (row_at(stop, half), q, r)).start()
+
+    def at_last():
+        return [(c, land(c, 2 + c, (row_at(0, half), q_down, r))) for c in range(2)]
+
+    def at_stop():
+        sides = (half, 1 - half)
+        return [
+            (2 * k + c, pass_on(2 * k + c, (row_at(near, sides[k]), q, r))) for c in range(2) for k in range(2)
+        ]
+
+    def at_near():
+        return [
+            (2 * k + c, land(2 * k + c, 4 + 2 * k + c, (row_at(0, half), q_down, r)))
+            for c in range(2) for k in range(2)
+        ]
+
+    places_on_way = ((last, at_last), (stop, at_stop), (near, at_near))
+
+    def forward():
+        for place, copies in places_on_way:
+            @pl.when(x == place)
+            def _():
+                for at, copy in copies():
+                    pass_on(at, away).wait_recv()
+                    copy.start()
+
+    def forwarded():
+        for place, copies in places_on_way:
+            @pl.when(x == place)
+            def _():
+                for _, copy in copies():
+                    copy.wait_send()
 
     sort_order(b_where, NB, rank, b_order)
     load_b.wait()
@@ -153,16 +237,16 @@
         return carry
 
     lax.fori_loop(0, NC, keep_first, 0)
-    firsts = []
-    for d in range(1, reps):
-        there = lax.rem(r + d, reps)
-        copy = pltpu.make_async_remote_copy(
-            src_ref=first.at[pl.ds(there * share, share)], dst_ref=got_first.at[d - 1],
-            send_sem=first_send.at[d - 1], recv_sem=first_recv.at[d - 1],
-            device_id=(p, q, there), device_id_type=MESH,
+    firsts = [
+        remote(
+            first.at[pl.ds(lax.rem(r + d, reps) * share, share)], got_first.at[d - 1],
+            first_send.at[d - 1], first_recv.at[d - 1], (p, q, lax.rem(r + d, reps)),
         )
+        for d in range(1, reps)
+    ]
+    for copy in firsts:
         copy.start()
-        firsts.append(copy)
+    forward()
 
     for copy in small:
         copy.wait_recv()
@@ -178,8 +262,14 @@
     for c in range(CHUNKS):
         panels[c].wait_recv()
         lax.fori_loop(c * PER_CHUNK, (c + 1) * PER_CHUNK, multiply(a_next), 0)
-    seconds = []
-    for d in range(reps):
+    seconds = [
+        remote(
+            second.at[pl.ds(lax.rem(r + d, reps) * share, share)], got_second.at[d],
+            second_send.at[d], second_recv.at[d], (p_down, q, lax.rem(r + d, reps)),
+        )
+        for d in range(reps)
+    ]
+    for d in sorted(range(reps), key=lambda d: -min(d, reps - d)):
         there = lax.rem(r + d, reps)
 
         def keep_second(s, carry):
@@ -187,13 +277,7 @@
             return carry
 
         lax.fori_loop(0, share, keep_second, 0)
-        copy = pltpu.make_async_remote_copy(
-            src_ref=second.at[pl.ds(there * share, share)], dst_ref=got_second.at[d],
-            send_sem=second_send.at[d], recv_sem=second_recv.at[d],
-            device_id=(p_down, q, there), device_id_type=MESH,
-        )
-        copy.start()
-        seconds.append(copy)
+        seconds[d].start()
 
     total = first[pl.ds(r * share, share)]
     for d in range(1, reps):
@@ -203,6 +287,7 @@
         seconds[d].wait_recv()
         total += got_second[d]
     out[...] = total
+    forwarded()
     for copy in small + panels + firsts + seconds:
         copy.wait_send()
 
@@ -224,6 +309,7 @@
             pltpu.VMEM((NA, BLOCK, BLOCK), f32),
             pltpu.VMEM((NB, BLOCK, BLOCK), f32),
             pltpu.VMEM((NA, BLOCK, BLOCK), f32),
+            pltpu.VMEM((NA // 2, BLOCK, BLOCK), f32),
             pltpu.VMEM((1, NA), i32),
             pltpu.VMEM((1, NC), i32),
             pltpu.SMEM((1, NA), i32),
@@ -232,14 +318,15 @@
             pltpu.VMEM((NA * CB, BLOCK, BLOCK), f32),
             pltpu.VMEM((NC, BLOCK, BLOCK), f32),
             pltpu.VMEM((NC, BLOCK, BLOCK), f32),
-            pltpu.VMEM((reps - 1, share, BLOCK, BLOCK), f32),
+            pltpu.VMEM((max(reps - 1, 1), share, BLOCK, BLOCK), f32),
             pltpu.VMEM((reps, share, BLOCK, BLOCK), f32),
             pltpu.SMEM((NB,), i32),
             pltpu.SMEM((NA,), i32),
             pltpu.SMEM((NB,), i32),
             pltpu.SMEM((NA,), i32),
             dma((2,)), dma((2,)), dma((2,)), dma((2,)), dma((CHUNKS,)), dma((CHUNKS,)),
-            dma((reps - 1,)), dma((reps - 1,)), dma((reps,)), dma((reps,)),
+            dma((CHUNKS // 2,)), dma((CHUNKS // 2,)),
+            dma((max(reps - 1, 1),)), dma((max(reps - 1, 1),)), dma((reps,)), dma((reps,)),
         ],
         compiler_params=pltpu.CompilerParams(
             collective_id=0, has_side_effects=True, vmem_limit_bytes=60 * 1024 * 1024

time: 95.7 us -> 69.6 us (0.73)
  Pallas kernels: 94 us -> 67.9 us
    pallas_call x1, Pallas kernels: 94 us -> 67.9 us  [shards(): pl.pallas_call(functools.partial(kernel, rows, cols, reps), out_shape=jax...]
where the time goes in v2:
time: 69.6 us; the launch traced here: 69.4 us
  Pallas kernels  67.9 us (98%)
  local copies, waits for them, and re-layouts  1.57 us (2%)
    pallas_call x1, Pallas kernels, shards(): pl.pallas_call(functools.partial(kernel, rows, cols, reps), out_shape=jax...  67.9 us
    unnamed x1, local copies, waits for them, and re-layouts  1.57 us

profile of v2, /device:TPU:399, one launch (start us, length us, event | category | flops | bytes accessed | tf_op | source)
XLA Modules:
  0.0 69.4 jit_solution(1149776181795361519)
XLA Ops:
  0.0 67.9 %shard_map.55 = f32[2,128,128]{2,1,0:T(8,128)} custom-call(s32[1,16]{1,0:T(1,128)} %bitcast.9, s32[1,32]{1,0:T(1,128)} %bitcast.11, s32[1,8]{1,0:T(1,128)} %bitcast.12, f32[16,128,128]{2,1,0:T(8,128)} %bitcast.8, f32[32,128,128]{2,1,0:T(8,128)} %bitcast.7, s32[1,16]{1,0:T(1,128)} %bitcast.10, s32[1,8]{1,0:T(1,128)} %bitcast.13), custom_call_target="tpu_custom_call" | custom-call | flops 2147483648 | bytes 4194304 | tf_op jit(solution)/shard_map/pallas_call | solution.py:303
  67.9 1.6 %copy.7 = f32[1,1,2,128,128]{4,3,2,1,0:T(8,128)} copy(f32[1,1,2,128,128]{4,3,2,1,0:T(8,128)} %bitcast.6) | data formatting | bytes 262144

commit v3 on v2

--- a/solution.py
+++ b/solution.py
@@ -17,6 +17,9 @@
 BLOCK = 128
 CHUNKS = 8
 PER_CHUNK = NA // CHUNKS
+STRAIGHT = 2
+WAYS = (((3,), 3), ((7,), 3))
+RELAYED = (1, 2)
 MESH = pl.DeviceIdType.MESH
 
 
@@ -50,9 +53,9 @@
 def kernel(
     rows, cols, reps,
     a_where, b_where, c_where, a_hbm, b_hbm, aw_hbm, cw_hbm, out,
-    a_own, b_own, a_next, via, aw_land, cw_land, aw_next, cw_next, right, pieces, first, second, got_first, got_second,
+    a_own, b_own, a_next, via, aw_land, cw_land, aw_next, cw_next, right, pieces, first, second, got_first, got_second, relay, relay_sum,
     rank, a_order, b_order, inner,
-    local_sem, meta_sem, small_send, small_recv, a_send, a_recv, via_send, via_recv, first_send, first_recv, second_send, second_recv,
+    local_sem, meta_sem, small_send, small_recv, a_send, a_recv, via_send, via_recv, first_send, first_recv, second_send, second_recv, relay_out, relay_recv, relay_send, relay_landed,
 ):
     p, q, r = lax.axis_index("row"), lax.axis_index("col"), lax.axis_index("rep")
     p_up, p_down = lax.rem(p + 1, rows), lax.rem(p + rows - 1, rows)
@@ -66,7 +69,12 @@
 
     width = rows // 2
     x, half = lax.rem(p, width), p // width
-    last, stop, near = width - 1, width // 2, width // 8
+    last = width - 1
+    ways, taken = [], STRAIGHT
+    for stops, count in WAYS:
+        ways.append((stops, taken, count))
+        taken += count
+    relayed = (r == RELAYED[0]) | (r == RELAYED[1])
     across = lax.rem(p + width, rows)
 
     def row_at(at, side):
@@ -90,26 +98,33 @@
         if d:
             greet(p, q, there)
 
-    @pl.when(x == last)
-    def _():
-        greet(across, q, r)
-
-    @pl.when(x == stop)
-    def _():
-        greet(row_at(last, 0), q, r)
-        greet(row_at(last, 1), q, r)
-
-    @pl.when(x == near)
-    def _():
-        greet(row_at(stop, 0), q, r)
-        greet(row_at(stop, 1), q, r)
+    far_side = 1 - half
+
+    for stops, _, _ in ways:
+        for n, place in enumerate(stops):
+            @pl.when(x == place)
+            def _():
+                greet(row_at(stops[n - 1], half) if n else row_at(last, far_side), q, r)
 
     @pl.when(x == 0)
     def _():
-        greet(row_at(last, half), q_up, r)
-        greet(row_at(near, half), q_up, r)
-
-    more = jnp.where(x == last, 4, jnp.where(x == stop, 2, jnp.where(x == near, 1, 0)))
+        for stops, _, _ in ways:
+            greet(row_at(stops[-1], half), q_up, r)
+
+    @pl.when((x == 0) & relayed)
+    def _():
+        for d in range(reps):
+            greet(across, q, lax.rem(r + d, reps))
+
+    @pl.when((x == last) & relayed)
+    def _():
+        greet(row_at(0, half), q, r)
+
+    more = jnp.where(x == last, len(ways), 0)
+    for stops, _, _ in ways:
+        for place in stops:
+            more += jnp.where(x == place, 1, 0)
+    more += jnp.where(x == 0, len(RELAYED), 0) + jnp.where((x == 0) & relayed, 1, 0)
     pl.semaphore_wait(barrier, 2 * reps + 1 + more)
 
     away = (p_up, q_down, r)
@@ -133,53 +148,46 @@
     def pass_on(at, device):
         return remote(via.at[part(at)], via.at[part(at)], via_send.at[at], via_recv.at[at], device)
 
-    def land(at, c, device):
-        return remote(via.at[part(at)], a_next.at[part(c)], via_send.at[at], a_recv.at[c], device)
+    def land(at, c):
+        return remote(
+            via.at[part(at)], a_next.at[part(c)], via_send.at[at], a_recv.at[c], (row_at(0, half), q_down, r)
+        )
 
     @pl.when(x != last)
     def _():
         for copy in panels:
             copy.start()
 
-    @pl.when(x == last)
-    def _():
-        for c in range(2):
-            panels[c].start()
-            leg(2 + c, c, (across, q, r)).start()
-            leg(4 + c, c, (row_at(stop, 1 - half), q, r)).start()
-            leg(6 + c, 2 + c, (row_at(stop, half), q, r)).start()
-
-    def at_last():
-        return [(c, land(c, 2 + c, (row_at(0, half), q_down, r))) for c in range(2)]
-
-    def at_stop():
-        sides = (half, 1 - half)
-        return [
-            (2 * k + c, pass_on(2 * k + c, (row_at(near, sides[k]), q, r))) for c in range(2) for k in range(2)
-        ]
-
-    def at_near():
-        return [
-            (2 * k + c, land(2 * k + c, 4 + 2 * k + c, (row_at(0, half), q_down, r)))
-            for c in range(2) for k in range(2)
-        ]
-
-    places_on_way = ((last, at_last), (stop, at_stop), (near, at_near))
+    def send_around(at):
+        @pl.when(x == last)
+        def _():
+            for stops, start, count in ways:
+                if at < count:
+                    leg(start + at, at, (row_at(stops[0], far_side), q, r)).start()
+            if at < STRAIGHT:
+                panels[at].start()
+
+    send_around(0)
+
+    def next_leg(n, stops, at, c):
+        return pass_on(at, (row_at(stops[n + 1], half), q, r)) if n + 1 < len(stops) else land(at, c)
 
     def forward():
-        for place, copies in places_on_way:
-            @pl.when(x == place)
-            def _():
-                for at, copy in copies():
-                    pass_on(at, away).wait_recv()
-                    copy.start()
+        for stops, start, count in ways:
+            for n, place in enumerate(stops):
+                @pl.when(x == place)
+                def _():
+                    for at in range(count):
+                        pass_on(at, away).wait_recv()
+                        next_leg(n, stops, at, start + at).start()
 
     def forwarded():
-        for place, copies in places_on_way:
-            @pl.when(x == place)
-            def _():
-                for _, copy in copies():
-                    copy.wait_send()
+        for stops, start, count in ways:
+            for n, place in enumerate(stops):
+                @pl.when(x == place)
+                def _():
+                    for at in range(count):
+                        next_leg(n, stops, at, start + at).wait_send()
 
     sort_order(b_where, NB, rank, b_order)
     load_b.wait()
@@ -193,6 +201,7 @@
         return carry
 
     lax.fori_loop(0, KSET, lay_right, 0)
+    send_around(1)
 
     def places(where):
         def one(n, carry):
@@ -230,7 +239,9 @@
 
     places(a_where)
     load_a.wait()
-    lax.fori_loop(0, NA, multiply(a_own), 0)
+    lax.fori_loop(0, NA // 2, multiply(a_own), 0)
+    send_around(2)
+    lax.fori_loop(NA // 2, NA, multiply(a_own), 0)
 
     def keep_first(s, carry):
         keep(c_where, first, s)
@@ -244,9 +255,12 @@
         )
         for d in range(1, reps)
     ]
-    for copy in firsts:
-        copy.start()
     forward()
+
+    @pl.when(x != 0)
+    def _():
+        for copy in firsts:
+            copy.start()
 
     for copy in small:
         copy.wait_recv()
@@ -262,33 +276,91 @@
     for c in range(CHUNKS):
         panels[c].wait_recv()
         lax.fori_loop(c * PER_CHUNK, (c + 1) * PER_CHUNK, multiply(a_next), 0)
-    seconds = [
-        remote(
-            second.at[pl.ds(lax.rem(r + d, reps) * share, share)], got_second.at[d],
+        if c == STRAIGHT - 1:
+            @pl.when(x == 0)
+            def _():
+                for copy in firsts:
+                    copy.start()
+    def straight_back(d, count):
+        return remote(
+            second.at[pl.ds(lax.rem(r + d, reps) * share, count)], got_second.at[d, pl.ds(0, count)],
             second_send.at[d], second_recv.at[d], (p_down, q, lax.rem(r + d, reps)),
         )
-        for d in range(reps)
-    ]
+
+    def to_relay(d):
+        return remote(
+            second.at[pl.ds(lax.rem(r + d, reps) * share + share - 1, 1)], relay.at[d],
+            relay_out.at[d], relay_recv.at[d], (across, q, lax.rem(r + d, reps)),
+        )
+
+    def turned(d):
+        there = lax.rem(r + d, reps)
+        return (x == 0) & ((there == RELAYED[0]) | (there == RELAYED[1]))
+
+    relay_on = remote(
+        relay_sum, got_second.at[0, pl.ds(share - 1, 1)], relay_send, relay_landed, (row_at(0, half) + last, q, r)
+    )
     for d in sorted(range(reps), key=lambda d: -min(d, reps - d)):
         there = lax.rem(r + d, reps)
-
         def keep_second(s, carry):
             keep(cw_next, second, there * share + s)
             return carry
 
         lax.fori_loop(0, share, keep_second, 0)
-        seconds[d].start()
-
-    total = first[pl.ds(r * share, share)]
+
+        @pl.when(turned(d))
+        def _():
+            to_relay(d).start()
+            straight_back(d, share - 1).start()
+
+        @pl.when(jnp.logical_not(turned(d)))
+        def _():
+            straight_back(d, share).start()
+
+    @pl.when((x == 0) & relayed)
+    def _():
+        to_relay(0).wait_recv()
+        relay_sum[...] = relay[0]
+        for d in range(1, reps):
+            to_relay(d).wait_recv()
+            relay_sum[...] += relay[d]
+        relay_on.start()
+
+    out[...] = first[pl.ds(r * share, share)]
     for d in range(1, reps):
         firsts[d - 1].wait_recv()
-        total += got_first[d - 1]
+        out[...] += got_first[d - 1]
+
+    @pl.when((x == last) & relayed)
+    def _():
+        for d in range(reps):
+            straight_back(d, share - 1).wait_recv()
+            out[:share - 1] += got_second[d, :share - 1]
+        relay_on.wait_recv()
+        out[share - 1:] += got_second[0, share - 1:]
+
+    @pl.when(jnp.logical_not((x == last) & relayed))
+    def _():
+        for d in range(reps):
+            straight_back(d, share).wait_recv()
+            out[...] += got_second[d]
+
+    @pl.when((x == 0) & relayed)
+    def _():
+        relay_on.wait_send()
+
     for d in range(reps):
-        seconds[d].wait_recv()
-        total += got_second[d]
-    out[...] = total
+        @pl.when(turned(d))
+        def _():
+            to_relay(d).wait_send()
+            straight_back(d, share - 1).wait_send()
+
+        @pl.when(jnp.logical_not(turned(d)))
+        def _():
+            straight_back(d, share).wait_send()
+
     forwarded()
-    for copy in small + panels + firsts + seconds:
+    for copy in small + panels + firsts:
         copy.wait_send()
 
 
@@ -309,7 +381,7 @@
             pltpu.VMEM((NA, BLOCK, BLOCK), f32),
             pltpu.VMEM((NB, BLOCK, BLOCK), f32),
             pltpu.VMEM((NA, BLOCK, BLOCK), f32),
-            pltpu.VMEM((NA // 2, BLOCK, BLOCK), f32),
+            pltpu.VMEM((max(count for _, count in WAYS) * PER_CHUNK, BLOCK, BLOCK), f32),
             pltpu.VMEM((1, NA), i32),
             pltpu.VMEM((1, NC), i32),
             pltpu.SMEM((1, NA), i32),
@@ -320,13 +392,15 @@
             pltpu.VMEM((NC, BLOCK, BLOCK), f32),
             pltpu.VMEM((max(reps - 1, 1), share, BLOCK, BLOCK), f32),
             pltpu.VMEM((reps, share, BLOCK, BLOCK), f32),
+            pltpu.VMEM((reps, 1, BLOCK, BLOCK), f32),
+            pltpu.VMEM((1, BLOCK, BLOCK), f32),
             pltpu.SMEM((NB,), i32),
             pltpu.SMEM((NA,), i32),
             pltpu.SMEM((NB,), i32),
             pltpu.SMEM((NA,), i32),
             dma((2,)), dma((2,)), dma((2,)), dma((2,)), dma((CHUNKS,)), dma((CHUNKS,)),
-            dma((CHUNKS // 2,)), dma((CHUNKS // 2,)),
-            dma((max(reps - 1, 1),)), dma((max(reps - 1, 1),)), dma((reps,)), dma((reps,)),
+            dma((max(count for _, count in WAYS),)), dma((max(count for _, count in WAYS),)),
+            dma((max(reps - 1, 1),)), dma((max(reps - 1, 1),)), dma((reps,)), dma((reps,)), dma((reps,)), dma((reps,)), dma, dma,
         ],
         compiler_params=pltpu.CompilerParams(
             collective_id=0, has_side_effects=True, vmem_limit_bytes=60 * 1024 * 1024

time: 69.6 us -> 64.2 us (0.922)
  the two profiles are of different devices: /device:TPU:399 before, /device:TPU:655 now
where the time goes in v3:
time: 64.2 us; the launch traced here: 64 us
  Pallas kernels  62.5 us (97%)
  local copies, waits for them, and re-layouts  1.57 us (2%)
    pallas_call x1, Pallas kernels, shards(): pl.pallas_call(functools.partial(kernel, rows, cols, reps), out_shape=jax...  62.5 us
    unnamed x1, local copies, waits for them, and re-layouts  1.57 us

profile of v3, /device:TPU:655, one launch (start us, length us, event | category | flops | bytes accessed | tf_op | source)
XLA Modules:
  0.0 64.0 jit_solution(924890132862735505)
XLA Ops:
  0.0 62.5 %shard_map.55 = f32[2,128,128]{2,1,0:T(8,128)} custom-call(s32[1,16]{1,0:T(1,128)} %bitcast.9, s32[1,32]{1,0:T(1,128)} %bitcast.11, s32[1,8]{1,0:T(1,128)} %bitcast.12, f32[16,128,128]{2,1,0:T(8,128)} %bitcast.8, f32[32,128,128]{2,1,0:T(8,128)} %bitcast.7, s32[1,16]{1,0:T(1,128)} %bitcast.10, s32[1,8]{1,0:T(1,128)} %bitcast.13), custom_call_target="tpu_custom_call" | custom-call | flops 2147483648 | bytes 4194304 | tf_op jit(solution)/shard_map/pallas_call | solution.py:375
  62.5 1.6 %copy.7 = f32[1,1,2,128,128]{4,3,2,1,0:T(8,128)} copy(f32[1,1,2,128,128]{4,3,2,1,0:T(8,128)} %bitcast.6) | data formatting | bytes 262144

commit v4 on v3

--- a/solution.py
+++ b/solution.py
@@ -18,7 +18,7 @@
 CHUNKS = 8
 PER_CHUNK = NA // CHUNKS
 STRAIGHT = 2
-WAYS = (((3,), 3), ((7,), 3))
+WAYS = (((7,), 3), ((3,), 3))
 RELAYED = (1, 2)
 MESH = pl.DeviceIdType.MESH
 
@@ -74,7 +74,13 @@
     for stops, count in WAYS:
         ways.append((stops, taken, count))
         taken += count
-    relayed = (r == RELAYED[0]) | (r == RELAYED[1])
+    beside = last - 1
+
+    def is_relayed(rep):
+        return functools.reduce(jnp.logical_or, [rep == one for one in RELAYED])
+
+    relayed = is_relayed(r)
+    relaying = ((x == 0) & relayed) | ((x == beside) & jnp.logical_not(relayed))
     across = lax.rem(p + width, rows)
 
     def row_at(at, side):
@@ -111,20 +117,20 @@
         for stops, _, _ in ways:
             greet(row_at(stops[-1], half), q_up, r)
 
-    @pl.when((x == 0) & relayed)
+    @pl.when(relaying)
     def _():
         for d in range(reps):
-            greet(across, q, lax.rem(r + d, reps))
-
-    @pl.when((x == last) & relayed)
-    def _():
-        greet(row_at(0, half), q, r)
+            greet(row_at(0, far_side), q, lax.rem(r + d, reps))
+
+    @pl.when(x == last)
+    def _():
+        greet(row_at(jnp.where(relayed, 0, beside), half), q, r)
 
     more = jnp.where(x == last, len(ways), 0)
     for stops, _, _ in ways:
         for place in stops:
             more += jnp.where(x == place, 1, 0)
-    more += jnp.where(x == 0, len(RELAYED), 0) + jnp.where((x == 0) & relayed, 1, 0)
+    more += jnp.where(x == 0, reps, 0) + jnp.where(relaying, 1, 0)
     pl.semaphore_wait(barrier, 2 * reps + 1 + more)
 
     away = (p_up, q_down, r)
@@ -288,17 +294,14 @@
         )
 
     def to_relay(d):
+        there = lax.rem(r + d, reps)
         return remote(
-            second.at[pl.ds(lax.rem(r + d, reps) * share + share - 1, 1)], relay.at[d],
-            relay_out.at[d], relay_recv.at[d], (across, q, lax.rem(r + d, reps)),
+            second.at[pl.ds(there * share + share - 1, 1)], relay.at[d], relay_out.at[d], relay_recv.at[d],
+            (row_at(jnp.where(is_relayed(there), 0, beside), far_side), q, there),
         )
 
-    def turned(d):
-        there = lax.rem(r + d, reps)
-        return (x == 0) & ((there == RELAYED[0]) | (there == RELAYED[1]))
-
     relay_on = remote(
-        relay_sum, got_second.at[0, pl.ds(share - 1, 1)], relay_send, relay_landed, (row_at(0, half) + last, q, r)
+        relay_sum, got_second.at[0, pl.ds(share - 1, 1)], relay_send, relay_landed, (row_at(last, half), q, r)
     )
     for d in sorted(range(reps), key=lambda d: -min(d, reps - d)):
         there = lax.rem(r + d, reps)
@@ -308,16 +311,16 @@
 
         lax.fori_loop(0, share, keep_second, 0)
 
-        @pl.when(turned(d))
+        @pl.when(x == 0)
         def _():
             to_relay(d).start()
             straight_back(d, share - 1).start()
 
-        @pl.when(jnp.logical_not(turned(d)))
+        @pl.when(x != 0)
         def _():
             straight_back(d, share).start()
 
-    @pl.when((x == 0) & relayed)
+    @pl.when(relaying)
     def _():
         to_relay(0).wait_recv()
         relay_sum[...] = relay[0]
@@ -331,7 +334,7 @@
         firsts[d - 1].wait_recv()
         out[...] += got_first[d - 1]
 
-    @pl.when((x == last) & relayed)
+    @pl.when(x == last)
     def _():
         for d in range(reps):
             straight_back(d, share - 1).wait_recv()
@@ -339,23 +342,23 @@
         relay_on.wait_recv()
         out[share - 1:] += got_second[0, share - 1:]
 
-    @pl.when(jnp.logical_not((x == last) & relayed))
+    @pl.when(x != last)
     def _():
         for d in range(reps):
             straight_back(d, share).wait_recv()
             out[...] += got_second[d]
 
-    @pl.when((x == 0) & relayed)
+    @pl.when(relaying)
     def _():
         relay_on.wait_send()
 
     for d in range(reps):
-        @pl.when(turned(d))
+        @pl.when(x == 0)
         def _():
             to_relay(d).wait_send()
             straight_back(d, share - 1).wait_send()
 
-        @pl.when(jnp.logical_not(turned(d)))
+        @pl.when(x != 0)
         def _():
             straight_back(d, share).wait_send()
 

time: 64.2 us -> 61.2 us (0.953)
  the two profiles are of different devices: /device:TPU:655 before, /device:TPU:783 now
where the time goes in v4:
time: 61.2 us; the launch traced here: 61 us
  Pallas kernels  59.5 us (97%)
  local copies, waits for them, and re-layouts  1.57 us (3%)
    pallas_call x1, Pallas kernels, shards(): pl.pallas_call(functools.partial(kernel, rows, cols, reps), out_shape=jax...  59.5 us
    unnamed x1, local copies, waits for them, and re-layouts  1.57 us

profile of v4, /device:TPU:783, one launch (start us, length us, event | category | flops | bytes accessed | tf_op | source)
XLA Modules:
  0.0 61.0 jit_solution(6812333321775830827)
XLA Ops:
  0.0 59.5 %shard_map.55 = f32[2,128,128]{2,1,0:T(8,128)} custom-call(s32[1,16]{1,0:T(1,128)} %bitcast.9, s32[1,32]{1,0:T(1,128)} %bitcast.11, s32[1,8]{1,0:T(1,128)} %bitcast.12, f32[16,128,128]{2,1,0:T(8,128)} %bitcast.8, f32[32,128,128]{2,1,0:T(8,128)} %bitcast.7, s32[1,16]{1,0:T(1,128)} %bitcast.10, s32[1,8]{1,0:T(1,128)} %bitcast.13), custom_call_target="tpu_custom_call" | custom-call | flops 2147483648 | bytes 4194304 | tf_op jit(solution)/shard_map/pallas_call | solution.py:378
  59.5 1.6 %copy.7 = f32[1,1,2,128,128]{4,3,2,1,0:T(8,128)} copy(f32[1,1,2,128,128]{4,3,2,1,0:T(8,128)} %bitcast.6) | data formatting | bytes 262144

commit v5 on v4

--- a/solution.py
+++ b/solution.py
@@ -15,11 +15,11 @@
 NB = 32
 NC = 8
 BLOCK = 128
-CHUNKS = 8
+CHUNKS = 16
 PER_CHUNK = NA // CHUNKS
-STRAIGHT = 2
-WAYS = (((7,), 3), ((3,), 3))
-RELAYED = (1, 2)
+STRAIGHT = 5
+WAYS = (((7,), 6), ((3,), 5))
+RELAYED = (1,)
 MESH = pl.DeviceIdType.MESH
 
 
@@ -164,14 +164,15 @@
         for copy in panels:
             copy.start()
 
-    def send_around(at):
+    def send_around(turn):
         @pl.when(x == last)
         def _():
-            for stops, start, count in ways:
-                if at < count:
-                    leg(start + at, at, (row_at(stops[0], far_side), q, r)).start()
-            if at < STRAIGHT:
-                panels[at].start()
+            for at in range(2 * turn, 2 * turn + 2):
+                for stops, start, count in ways:
+                    if at < count:
+                        leg(start + at, at, (row_at(stops[0], far_side), q, r)).start()
+                if at < STRAIGHT:
+                    panels[at].start()
 
     send_around(0)
 

time: 61.2 us -> 61.8 us (level)
  the two profiles are of different devices: /device:TPU:783 before, /device:TPU:17 now
where the time goes in v5:
time: 61.8 us; the launch traced here: 61.6 us
  Pallas kernels  60 us (97%)
  local copies, waits for them, and re-layouts  1.57 us (3%)
    pallas_call x1, Pallas kernels, shards(): pl.pallas_call(functools.partial(kernel, rows, cols, reps), out_shape=jax...  60 us
    unnamed x1, local copies, waits for them, and re-layouts  1.57 us

profile of v5, /device:TPU:17, one launch (start us, length us, event | category | flops | bytes accessed | tf_op | source)
XLA Modules:
  0.0 61.6 jit_solution(15975863306340521843)
XLA Ops:
  0.0 60.0 %shard_map.55 = f32[2,128,128]{2,1,0:T(8,128)} custom-call(s32[1,16]{1,0:T(1,128)} %bitcast.9, s32[1,32]{1,0:T(1,128)} %bitcast.11, s32[1,8]{1,0:T(1,128)} %bitcast.12, f32[16,128,128]{2,1,0:T(8,128)} %bitcast.8, f32[32,128,128]{2,1,0:T(8,128)} %bitcast.7, s32[1,16]{1,0:T(1,128)} %bitcast.10, s32[1,8]{1,0:T(1,128)} %bitcast.13), custom_call_target="tpu_custom_call" | custom-call | flops 2147483648 | bytes 4194304 | tf_op jit(solution)/shard_map/pallas_call | solution.py:379
  60.0 1.6 %copy.7 = f32[1,1,2,128,128]{4,3,2,1,0:T(8,128)} copy(f32[1,1,2,128,128]{4,3,2,1,0:T(8,128)} %bitcast.6) | data formatting | bytes 262144
